TPU v7x, 512 devices: a whole 4x8x8 slice. The times are simulated.
512 devices in a mesh: pipe: 8 (over z), expert: 64 (over x, y, core).
Axes of the slice: x: 4, y: 8, z: 8, core: 2. Of those that a mesh axis runs over, the one named last changes fastest.
Arguments:
- state_down: bfloat16 [8, 1024, 3584], P('pipe', 'expert'), may hold values from -6 to 6
- state_up: bfloat16 [8, 1024, 3584], P('pipe', 'expert'), may hold values from -6 to 6
- routes: int32 [1, 8, 2, 1024, 2], P(None, 'pipe', None, 'expert'), may hold values from 0 to 7, all different within a row; in each aligned block of 16 rows (0 to 15, 16 to 31, ..., all dimensions but the last counted through in order) at most 8 rows name the same one
- gains: float32 [8, 2, 3584], P('pipe'), may hold values from 0.1 to 1.9
- router: bfloat16 [8, 2, 3584, 8], P('pipe'), may hold values from -0.09375 to 0.09375
- w_up: bfloat16 [8, 2, 3584, 8192], P('pipe', None, None, 'expert'), may hold values from -0.09375 to 0.09375
- w_down: bfloat16 [8, 2, 8192, 3584], P('pipe', None, 'expert'), may hold values from -0.1875 to 0.1875
Outputs:
- new_down: bfloat16 [8, 1024, 3584], P('pipe', 'expert')
- new_up: bfloat16 [8, 1024, 3584], P('pipe', 'expert')
Inputs may be any that keep to these rules, and one draw needn't show every extreme that they name: `routes`: each row names 2 different experts. Among the 16 tokens of one index of expert (aligned blocks) for one step, pipe index and side, no expert is named by more than 8 tokens, a bound that some block reaches.
All inputs are finite; a program needn't handle non-finite values.
Results may differ from a plain program's by a relative error of at most 0.009.
Values may be sent and summed in bfloat16 or wider, within the bound.
A program may use at most 64 MiB of HBM per device.

v0:
```python
import jax
import jax.numpy as jnp
from jax import lax
from jax.sharding import PartitionSpec as P

epsilon = 1e-06
route_scale = 2.5


def shifted(shard, axis, by):
    size = lax.axis_size(axis)
    pairs = [(i, i + by) for i in range(size) if 0 <= i + by < size]
    return lax.ppermute(shard, axis, pairs)


def slot_table(token_routes, experts, capacity):
    flat_routes = token_routes.reshape(-1)
    expert_hit = (flat_routes[:, None] == jnp.arange(experts, dtype=jnp.int32)[None, :]).astype(
        jnp.int32
    )
    earlier = jnp.cumsum(expert_hit, axis=0) - expert_hit
    slot_index = jnp.sum(earlier * expert_hit, axis=1)
    slot_hit = (slot_index[:, None] == jnp.arange(capacity, dtype=jnp.int32)[None, :]).astype(
        jnp.int32
    )
    return (expert_hit[:, :, None] * slot_hit[:, None, :]).astype(jnp.float32)


def prepare(tokens, token_routes, gain_row, router, experts, capacity, split_count):
    feature_count = tokens.shape[-1]
    wide_tokens = tokens.astype(jnp.float32)
    scale_rows = lax.rsqrt(jnp.mean(wide_tokens * wide_tokens, axis=-1, keepdims=True) + epsilon)
    normed = (wide_tokens * scale_rows * gain_row).astype(jnp.bfloat16)
    logits = jnp.dot(normed, router, preferred_element_type=jnp.float32)
    expert_hit = (
        token_routes[:, :, None] == jnp.arange(experts, dtype=jnp.int32)[None, None, :]
    ).astype(jnp.float32)
    affinity = jax.nn.sigmoid(jnp.sum(expert_hit * logits[:, None, :], axis=-1))
    weight = route_scale * affinity / jnp.sum(affinity, axis=-1, keepdims=True)
    slot_map = slot_table(token_routes, experts, capacity)
    row_inputs = jnp.repeat(normed, token_routes.shape[1], axis=0)
    filled = jnp.einsum(
        "rec,rd->ecd", slot_map.astype(jnp.bfloat16), row_inputs, preferred_element_type=jnp.float32
    ).astype(jnp.bfloat16)
    send_rows = jnp.broadcast_to(filled[:, None], (experts, split_count, capacity, feature_count))
    send_rows = send_rows.reshape(experts * split_count, capacity, feature_count)
    return (send_rows, slot_map, weight)


def expert_apply(received, up_cols, down_rows):
    feature_count = received.shape[-1]
    flat_rows = received.reshape(-1, feature_count)
    hidden = jax.nn.silu(jnp.dot(flat_rows, up_cols, preferred_element_type=jnp.float32)).astype(
        jnp.bfloat16
    )
    partial_out = jnp.dot(hidden, down_rows, preferred_element_type=jnp.float32).astype(
        jnp.bfloat16
    )
    return partial_out.reshape(received.shape)


def finish(tokens, returned, slot_map, weight, experts, split_count):
    feature_count = tokens.shape[-1]
    capacity = returned.shape[1]
    summed = jnp.sum(
        returned.reshape(experts, split_count, capacity, feature_count).astype(jnp.float32), axis=1
    )
    combined = jnp.einsum("rec,ecd->rd", slot_map, summed, precision=lax.Precision.HIGHEST)
    combined = combined.reshape(weight.shape[0], weight.shape[1], feature_count)
    branch_sum = jnp.sum(weight[:, :, None] * combined, axis=1)
    return (tokens.astype(jnp.float32) + branch_sum).astype(jnp.bfloat16)


def route_side(send_rows, up_cols, down_rows):
    answers = expert_apply(
        lax.all_to_all(send_rows, "expert", split_axis=0, concat_axis=0, tiled=True),
        up_cols,
        down_rows,
    )
    return lax.all_to_all(answers, "expert", split_axis=0, concat_axis=0, tiled=True)


def on_device(state_down, state_up, routes, gains, router, w_up, w_down):
    experts = router.shape[-1]
    split_count = lax.axis_size("expert") // experts
    tok_dev = state_down.shape[1]
    top_count = routes.shape[-1]
    capacity = min(tok_dev, max(2, 2 * tok_dev * top_count // experts))
    section_place = lax.axis_index("pipe")
    last_place = lax.axis_size("pipe") - 1
    down_state = state_down[0]
    up_state = state_up[0]
    down_send, down_map, down_weight = prepare(
        down_state, routes[0, 0, 0], gains[0, 0], router[0, 0], experts, capacity, split_count
    )
    up_send, up_map, up_weight = prepare(
        up_state, routes[0, 0, 1], gains[0, 1], router[0, 1], experts, capacity, split_count
    )
    down_back = route_side(down_send, w_up[0, 0], w_down[0, 0])
    up_back = route_side(up_send, w_up[0, 1], w_down[0, 1])
    down_out = finish(down_state, down_back, down_map, down_weight, experts, split_count)
    up_out = finish(up_state, up_back, up_map, up_weight, experts, split_count)
    from_lower = shifted(down_out, "pipe", 1)
    from_upper = shifted(up_out, "pipe", -1)
    down_state = jnp.where(section_place == 0, up_out, from_lower)
    up_state = jnp.where(section_place == last_place, down_out, from_upper)
    return (down_state[None], up_state[None])


def solution(mesh):
    in_specs = (
        P("pipe", "expert", None),
        P("pipe", "expert", None),
        P(None, "pipe", None, "expert", None),
        P("pipe", None, None),
        P("pipe", None, None, None),
        P("pipe", None, None, "expert"),
        P("pipe", None, "expert", None),
    )
    out_specs = (P("pipe", "expert", None), P("pipe", "expert", None))
    return jax.shard_map(
        on_device, mesh=mesh, in_specs=in_specs, out_specs=out_specs, check_vma=False
    )
```

profile of v0, /device:TPU:259, one launch (start us, length us, event | category | flops | bytes accessed | tf_op | source)
XLA Modules:
  0.0 391.6 jit_solution(1037812028969680950)
XLA Ops:
  0.6 0.7 slice_bitcast_fusion
  1.3 0.9 slice_reduce_fusion
  2.2 1.0 fusion.50
  3.3 1.0 fusion.44
  4.3 0.1 copy.21
  4.4 0.1 eq.133
  4.5 0.1 fusion.85
  4.6 0.1 copy.23
  4.7 0.2 select_reduce_fusion.1
  4.9 1.1 fusion.46
  6.0 0.1 broadcast_in_dim.12
  6.1 0.1 reshape.264
  6.2 0.2 convolution_convert_fusion.3
  6.5 2.1 broadcast_in_dim.13
  8.5 11.1 %all-to-all-start = ((bf16[64,8,3584]{2,1,0:T(8,128)(2,1)}), bf16[64,8,3584]{2,1,0:T(8,128)(2,1)}, u32[]{:S(2)}, u32[]{:S(2)}) async-start(bf16[64,8,3584]{2,1,0:T(8,128)(2,1)} %bitcast.125), calls=%async_computation | async-start | bytes 7340032 | tf_op jit(solution)/shard_map/all_to_all | solution.py:76
  19.7 0.1 copy.25
  19.8 0.1 eq.148
  19.9 0.1 fusion.82
  20.0 0.1 copy.27
  20.1 0.1 broadcast_in_dim.14
  20.2 0.1 reshape.267
  20.3 0.2 select_reduce_fusion
  20.5 0.3 convolution_convert_fusion.2
  20.7 83.4 %all-to-all-done = bf16[64,8,3584]{2,1,0:T(8,128)(2,1)} async-done(((bf16[64,8,3584]{2,1,0:T(8,128)(2,1)}), bf16[64,8,3584]{2,1,0:T(8,128)(2,1)}, u32[]{:S(2)}, u32[]{:S(2)}) %all-to-all-start) | async-done | bytes 3670048 | tf_op jit(solution)/shard_map/all_to_all | solution.py:76
  104.2 2.2 broadcast_in_dim.15
  106.4 6.2 %all-to-all-start.2 = ((bf16[64,8,3584]{2,1,0:T(8,128)(2,1)}), bf16[64,8,3584]{2,1,0:T(8,128)(2,1)}, u32[]{:S(2)}, u32[]{:S(2)}) async-start(bf16[64,8,3584]{2,1,0:T(8,128)(2,1)} %bitcast.126), calls=%async_computation.2 | async-start | bytes 7340032 | tf_op jit(solution)/shard_map/all_to_all | solution.py:76
  112.6 8.1 %fusion = bf16[64,8,3584]{2,1,0:T(8,128)(2,1)} fusion(bf16[1,2,128,3584]{3,2,1,0:T(8,128)(2,1)S(1)} %copy-done, bf16[1,2,3584,128]{3,2,1,0:T(8,128)(2,1)} %param.12, bf16[64,8,3584]{2,1,0:T(8,128)(2,1)} %all-to-all-done), kind=kOutput, calls=%fused_computation.4 | convolution fusion | flops 941686784 | bytes 9175040 | tf_op jit(solution)/shard_map/dot_general | solution.py:56
  120.7 76.4 %all-to-all-done.2 = bf16[64,8,3584]{2,1,0:T(8,128)(2,1)} async-done(((bf16[64,8,3584]{2,1,0:T(8,128)(2,1)}), bf16[64,8,3584]{2,1,0:T(8,128)(2,1)}, u32[]{:S(2)}, u32[]{:S(2)}) %all-to-all-start.2) | async-done | bytes 3670048 | tf_op jit(solution)/shard_map/all_to_all | solution.py:76
  197.1 6.1 %all-to-all-start.1 = ((bf16[64,8,3584]{2,1,0:T(8,128)(2,1)}), bf16[64,8,3584]{2,1,0:T(8,128)(2,1)}, u32[]{:S(2)}, u32[]{:S(2)}) async-start(bf16[64,8,3584]{2,1,0:T(8,128)(2,1)} %fusion), calls=%async_computation.1 | async-start | bytes 7340032 | tf_op jit(solution)/shard_map/all_to_all | solution.py:80
  203.2 8.1 %fusion.1 = bf16[64,8,3584]{2,1,0:T(8,128)(2,1)} fusion(bf16[1,2,128,3584]{3,2,1,0:T(8,128)(2,1)S(1)} %copy-done, bf16[1,2,3584,128]{3,2,1,0:T(8,128)(2,1)} %param.12, bf16[64,8,3584]{2,1,0:T(8,128)(2,1)} %all-to-all-done.2), kind=kOutput, calls=%fused_computation.5 | convolution fusion | flops 941686784 | bytes 9175040 | tf_op jit(solution)/shard_map/dot_general | solution.py:56
  211.3 76.4 %all-to-all-done.1 = bf16[64,8,3584]{2,1,0:T(8,128)(2,1)} async-done(((bf16[64,8,3584]{2,1,0:T(8,128)(2,1)}), bf16[64,8,3584]{2,1,0:T(8,128)(2,1)}, u32[]{:S(2)}, u32[]{:S(2)}) %all-to-all-start.1) | async-done | bytes 3670048 | tf_op jit(solution)/shard_map/all_to_all | solution.py:80
  287.7 6.1 %all-to-all-start.3 = ((bf16[64,8,3584]{2,1,0:T(8,128)(2,1)}), bf16[64,8,3584]{2,1,0:T(8,128)(2,1)}, u32[]{:S(2)}, u32[]{:S(2)}) async-start(bf16[64,8,3584]{2,1,0:T(8,128)(2,1)} %fusion.1), calls=%async_computation.3 | async-start | bytes 7340032 | tf_op jit(solution)/shard_map/all_to_all | solution.py:80
  293.8 0.1 eq.137
  293.8 0.1 eq.152
  293.9 0.1 copy.22
  294.0 0.1 copy.26
  294.1 0.2 fusion.59
  294.3 0.2 fusion.62
  294.7 2.6 convert_reduce_fusion.1
  297.3 1.1 fusion.8
  298.4 1.9 collective-permute-start.1
  300.4 77.9 %all-to-all-done.3 = bf16[64,8,3584]{2,1,0:T(8,128)(2,1)} async-done(((bf16[64,8,3584]{2,1,0:T(8,128)(2,1)}), bf16[64,8,3584]{2,1,0:T(8,128)(2,1)}, u32[]{:S(2)}, u32[]{:S(2)}) %all-to-all-start.3) | async-done | bytes 3670048 | tf_op jit(solution)/shard_map/all_to_all | solution.py:80
  378.3 2.6 convert_reduce_fusion
  380.9 1.1 fusion.9
  382.0 0.7 select_bitcast_fusion
  382.7 3.1 collective-permute-start
  385.8 5.1 %collective-permute-done = bf16[16,3584]{1,0:T(8,128)(2,1)S(1)} collective-permute-done((bf16[16,3584]{1,0:T(8,128)(2,1)S(1)}, bf16[16,3584]{1,0:T(8,128)(2,1)S(1)}, u32[]{:S(2)}, u32[]{:S(2)}) %collective-permute-start) | collective-permute-done | bytes 114720 | tf_op jit(solution)/shard_map/ppermute | solution.py:13
  390.9 0.7 select_bitcast_fusion.1
  (23 shorter events, 0.3 us)
Async XLA Ops:
  8.5 95.7 %all-to-all-start = ((bf16[64,8,3584]{2,1,0:T(8,128)(2,1)}), bf16[64,8,3584]{2,1,0:T(8,128)(2,1)}, u32[]{:S(2)}, u32[]{:S(2)}) async-start(bf16[64,8,3584]{2,1,0:T(8,128)(2,1)} %bitcast.125), calls=%async_computation | async-start | bytes 7340032 | tf_op jit(solution)/shard_map/all_to_all | solution.py:76
  106.4 6.2 %copy-start = (bf16[1,2,128,3584]{3,2,1,0:T(8,128)(2,1)S(1)}, bf16[1,2,128,3584]{3,2,1,0:T(8,128)(2,1)}, u32[]{:S(2)}) copy-start(bf16[1,2,128,3584]{3,2,1,0:T(8,128)(2,1)} %param.13) | copy-start | bytes 5505028
  106.4 90.7 %all-to-all-start.2 = ((bf16[64,8,3584]{2,1,0:T(8,128)(2,1)}), bf16[64,8,3584]{2,1,0:T(8,128)(2,1)}, u32[]{:S(2)}, u32[]{:S(2)}) async-start(bf16[64,8,3584]{2,1,0:T(8,128)(2,1)} %bitcast.126), calls=%async_computation.2 | async-start | bytes 7340032 | tf_op jit(solution)/shard_map/all_to_all | solution.py:76
  197.1 90.6 %all-to-all-start.1 = ((bf16[64,8,3584]{2,1,0:T(8,128)(2,1)}), bf16[64,8,3584]{2,1,0:T(8,128)(2,1)}, u32[]{:S(2)}, u32[]{:S(2)}) async-start(bf16[64,8,3584]{2,1,0:T(8,128)(2,1)} %fusion), calls=%async_computation.1 | async-start | bytes 7340032 | tf_op jit(solution)/shard_map/all_to_all | solution.py:80
  211.3 82.8 %copy-start.2 = (bf16[1,16,3584]{2,1,0:T(8,128)(2,1)S(1)}, bf16[1,16,3584]{2,1,0:T(8,128)(2,1)}, u32[]{:S(2)}) copy-start(bf16[1,16,3584]{2,1,0:T(8,128)(2,1)} %param.7) | copy-start | bytes 344068
  211.3 82.8 %copy-start.3 = (bf16[1,2,3584,8]{2,3,1,0:T(8,128)(2,1)S(1)}, bf16[1,2,3584,8]{2,3,1,0:T(8,128)(2,1)}, u32[]{:S(2)}) copy-start(bf16[1,2,3584,8]{2,3,1,0:T(8,128)(2,1)} %param.11) | copy-start | bytes 344068
  211.3 83.0 %copy-start.1 = (bf16[1,16,3584]{2,1,0:T(8,128)(2,1)S(1)}, bf16[1,16,3584]{2,1,0:T(8,128)(2,1)}, u32[]{:S(2)}) copy-start(bf16[1,16,3584]{2,1,0:T(8,128)(2,1)} %param.8) | copy-start | bytes 344068
  287.7 90.6 %all-to-all-start.3 = ((bf16[64,8,3584]{2,1,0:T(8,128)(2,1)}), bf16[64,8,3584]{2,1,0:T(8,128)(2,1)}, u32[]{:S(2)}, u32[]{:S(2)}) async-start(bf16[64,8,3584]{2,1,0:T(8,128)(2,1)} %fusion.1), calls=%async_computation.3 | async-start | bytes 7340032 | tf_op jit(solution)/shard_map/all_to_all | solution.py:80
  298.4 83.5 %collective-permute-start.1 = (bf16[16,3584]{1,0:T(8,128)(2,1)S(1)}, bf16[16,3584]{1,0:T(8,128)(2,1)S(1)}, u32[]{:S(2)}, u32[]{:S(2)}) collective-permute-start(bf16[16,3584]{1,0:T(8,128)(2,1)S(1)} %fusion.47), channel_id=1, source_target_pairs={{64,0},{128,64},{192,128},{256,192},{320,256},{384,320},{448,384},... | collective-permute-start | bytes 344072 | tf_op jit(solution)/shard_map/ppermute | solution.py:13
  382.7 8.2 %collective-permute-start = (bf16[16,3584]{1,0:T(8,128)(2,1)S(1)}, bf16[16,3584]{1,0:T(8,128)(2,1)S(1)}, u32[]{:S(2)}, u32[]{:S(2)}) collective-permute-start(bf16[16,3584]{1,0:T(8,128)(2,1)S(1)} %get-tuple-element.5), channel_id=1, source_target_pairs={{0,64},{64,128},{128,192},{192,256},{256,320},{320,384},{384,448},... | collective-permute-start | bytes 344072 | tf_op jit(solution)/shard_map/ppermute | solution.py:13
where the time goes:
time: 392 us
  waiting for transfers between devices  319 us (81%)
  starting transfers between devices  34.5 us (9%)
  matrix products  19.3 us (5%)
  other arithmetic  10.6 us (3%)
  local copies, waits for them, and re-layouts  7.07 us (2%)
    all_to_all x2, waiting for transfers between devices, route_side(): lax.all_to_all(send_rows, 'expert', split_axis=0, concat_axis=0, tiled=True)  160 us
    all_to_all x2, waiting for transfers between devices, route_side(): lax.all_to_all(answers, 'expert', split_axis=0, concat_axis=0, tiled=True)  154 us
    all_to_all x2, starting transfers between devices, route_side(): lax.all_to_all(send_rows, 'expert', split_axis=0, concat_axis=0, tiled=True)  17.3 us
    dot_general x2, matrix products, expert_apply(): jnp.dot(hidden, down_rows, preferred_element_type=jnp.float32)  16.2 us
    all_to_all x2, starting transfers between devices, route_side(): lax.all_to_all(answers, 'expert', split_axis=0, concat_axis=0, tiled=True)  12.2 us
  transfers between devices with their start and end apart: 6, of which 5 were waited for; matrix products, arithmetic and copies ran while one was open for 7% of the time, Pallas kernels for 0%

commit v1 on v0

v1 whole, which is shorter than its diff:
```python
import functools

import jax
import jax.numpy as jnp
from jax import lax
from jax.experimental import pallas as pl
from jax.experimental.pallas import tpu as pltpu
from jax.sharding import PartitionSpec as P

MESH = pl.DeviceIdType.MESH
EPSILON = 1e-06
ROUTE_SCALE = 2.5

NX, NY, NZ = 4, 8, 8
EXPERTS = 8
TOK = 16
CAP = 8
D = 3584
HALF = D // 2
META = 128
WIDE = D + META
TILE = 256
HID = 128
BLOCKS = NY
OWN = BLOCKS
LAG = 3

F32 = jnp.float32
BF16 = jnp.bfloat16


def dot(a, b):
    return jnp.dot(a, b, preferred_element_type=F32)


def dot_lanes(a, b):
    return lax.dot_general(a, b, (((1,), (1,)), ((), ())), preferred_element_type=F32)


def iota(shape, axis):
    return lax.broadcasted_iota(jnp.int32, shape, axis)


def kernel(
    down_ref, up_ref, routes_ref, gains_ref, router_ref, w_up_ref, w_down_ref,
    out_down, out_up,
    tok, sel, sel2, got, got2, ans, ans2, mate, sum2, back, back2, part, part_in, acc, wu, wd, fin, fin_in,
    own_send, a_send, a_recv, b_send, b_recv, f_send, f_recv, m_send, m_recv, d_send, d_recv,
    e_send, e_recv, w_local, w_send, w_recv, z_send, z_recv,
):
    z = lax.axis_index("pipe")
    place = lax.axis_index("expert")
    x = place // (2 * NY)
    y = lax.rem(place // 2, NY)
    core = lax.rem(place, 2)
    half_of_experts = y // (NY // 2)
    mine = lax.rem(y, 2)
    other = 1 - mine

    def at(dz=0, dx=0, dy=0):
        xx = lax.rem(x + dx + NX, NX)
        yy = lax.rem(y + dy + NY, NY)
        return (lax.rem(z + dz + NZ, NZ), (xx * NY + yy) * 2 + core)

    sibling = (z, place + 1 - 2 * core)
    pair = (z, place + 2 - 4 * mine)
    right, left = at(dy=1), at(dy=-1)

    def index_of(offset, parity):
        o = lax.rem(offset + parity + 2 * NY, NY)
        return jnp.where(o == 0, 0, jnp.where(o <= NY // 2, 2 * o - 1, 2 * (NY - o)))

    def index_at(position):
        return position + mine * (1 - 2 * lax.rem(position, 2))

    def offset_at(position):
        ahead = lax.rem(position + mine, 2)
        return (2 * ahead - 1) * ((position + 1) // 2)

    barrier = pltpu.get_barrier_semaphore()
    friends = (right, left, at(dx=1), at(dx=-1), at(dx=2), sibling, at(dz=1), at(dz=-1))
    for friend in friends:
        pl.semaphore_signal(barrier, inc=1, device_id=friend, device_id_type=MESH)

    def remote(src, dst, send, recv, device):
        return pltpu.make_async_remote_copy(
            src_ref=src, dst_ref=dst, send_sem=send, recv_sem=recv, device_id=device, device_id_type=MESH
        )

    def weight_views(index):
        side = index // 2
        if index % 2 == 0:
            return w_up_ref.at[0, side], [wu.at[:, pl.ds((2 * side + o) * HID, HID)] for o in (0, 1)]
        return w_down_ref.at[0, side], [wd.at[pl.ds((2 * side + o) * HID, HID), :] for o in (0, 1)]

    def weight_local(index):
        src, views = weight_views(index)
        return pltpu.make_async_copy(src, views[0], w_local.at[index])

    def weight_remote(index):
        src, views = weight_views(index)
        return remote(src, views[1], w_send.at[index], w_recv.at[index], sibling)

    for index in range(4):
        weight_local(index).start()

    expert_lane = iota((TOK, EXPERTS), 1)
    earlier = (iota((TOK, TOK), 1) < iota((TOK, TOK), 0)).astype(BF16)

    def put(first):
        return (iota((EXPERTS, META), 1) == iota((EXPERTS, META), 0) + first).astype(BF16)

    for side, state_ref in enumerate((down_ref, up_ref)):
        wide = state_ref[0].astype(F32)
        scale_rows = lax.rsqrt(jnp.mean(wide * wide, axis=-1, keepdims=True) + EPSILON)
        normed = (wide * scale_rows * gains_ref[0, side : side + 1, :]).astype(BF16)
        tok[mine, side, :, 0:D] = normed
        logits = dot_lanes(normed, router_ref[side])
        picked = routes_ref[side]
        hit = (picked[:, 0:1] == expert_lane) | (picked[:, 1:2] == expert_lane)
        affinity = jnp.where(hit, jax.nn.sigmoid(logits), 0.0)
        weight = ROUTE_SCALE * affinity / jnp.sum(affinity, axis=-1, keepdims=True)
        slot = dot(earlier, hit.astype(F32).astype(BF16))
        code = jnp.where(hit, slot, -1.0).astype(BF16)
        high = weight.astype(BF16)
        low = (weight - high.astype(F32)).astype(BF16)
        info = dot(code, put(0)) + dot(high, put(EXPERTS)) + dot(low, put(2 * EXPERTS))
        tok[mine, side, :, D:WIDE] = info.astype(BF16)

    pl.semaphore_wait(barrier, len(friends))

    def own_copy(way, side):
        into = index_of(1 - 2 * way, other)
        return remote(
            tok.at[mine, side], tok.at[into, side], own_send.at[way, side], a_recv.at[into, side],
            right if way else left,
        )

    for side in range(2):
        for way in range(2):
            own_copy(way, side).start()
    for index in range(4):
        weight_remote(index).start()

    zeros_half = jnp.zeros((TOK, HALF), BF16)
    for block in range(BLOCKS):
        back2[block, other] = zeros_half

    rows = 4 * TOK
    row = iota((rows, META), 0)
    expert_of_row = 2 * lax.rem(x + lax.shift_right_logical(row, 4), NX) + half_of_experts
    lane = iota((rows, META), 1)

    def spread(first):
        return (lane == expert_of_row + first).astype(BF16)

    def a_passed(position, side):
        ahead = lax.rem(position + mine, 2)
        last = 2 + (ahead if side else 1 - ahead)
        return (position >= 1) & ((position + 1) // 2 <= last)

    def a_copy(position, side):
        block, offset = index_at(position), offset_at(position)
        way = 1 - 2 * lax.rem(position + mine, 2)
        into = index_of(offset - way, other)
        return remote(
            tok.at[block, side], tok.at[into, side], a_send.at[block, side], a_recv.at[into, side], at(dy=way)
        )

    def a_wait(block, side):
        remote(
            tok.at[block, side], tok.at[block, side], a_send.at[block, side], a_recv.at[block, side], right
        ).wait_recv()

    def b_copy(block, kind):
        if kind == 2:
            src, dst = sel2.at[block, mine], got2.at[block, mine]
        else:
            src, dst = sel.at[block, kind], got.at[block, 1 + kind]
        return remote(src, dst, b_send.at[block, kind], b_recv.at[block, kind], at(dx=(1, -1, 2)[kind]))

    def f_copy(block):
        return remote(got2.at[block, mine], got2.at[block, mine], f_send.at[block], f_recv.at[block], pair)

    def f_wait(block):
        remote(
            got2.at[block, other], got2.at[block, other], f_send.at[block], f_recv.at[block], pair
        ).wait_recv()

    def m_copy(block):
        return remote(ans2.at[block, other], mate.at[block], m_send.at[block], m_recv.at[block], pair)

    def d_copy(block, kind):
        if kind == 2:
            src, dst = sum2.at[block], back2.at[block, mine]
        else:
            src, dst = ans.at[block, kind], back.at[block, 1 + kind]
        return remote(src, dst, d_send.at[block, kind], d_recv.at[block, kind], at(dx=(-1, 1, 2)[kind]))

    def choose(block):
        info = tok[block, :, :, D:WIDE].reshape(2 * TOK, META)
        code = dot_lanes(spread(0), info)
        r = iota((rows, 2 * TOK), 0)
        c = iota((rows, 2 * TOK), 1)
        hit = (code == (r & 7).astype(F32)) & ((lax.shift_right_logical(r, 3) & 1) == lax.shift_right_logical(c, 4))
        table = hit.astype(F32).astype(BF16)
        for first in range(0, D, TILE):
            span = slice(first, first + TILE)
            picked = dot(table, tok[block, :, :, span].reshape(2 * TOK, TILE)).astype(BF16)
            got[block, 0, :, span] = picked[0:TOK]
            sel[block, 0, :, span] = picked[TOK : 2 * TOK]
            inner = first % HALF
            sel2[block, first // HALF, :, inner : inner + TILE] = picked[2 * TOK : 3 * TOK]
            sel[block, 1, :, span] = picked[3 * TOK :]

    def experts(block):
        total = jnp.zeros((rows, 4 * HID), F32)
        for part_index in range(2):
            span = slice(part_index * HALF, (part_index + 1) * HALF)
            lhs = jnp.concatenate(
                [got[block, 0, :, span], got[block, 1, :, span], got2[block, part_index], got[block, 2, :, span]], axis=0
            )
            total = total + dot(lhs, wu[span, :])
        hidden = total * jax.nn.sigmoid(total)
        r = iota((rows, 4 * HID), 0)
        c = iota((rows, 4 * HID), 1)
        own_side = (lax.shift_right_logical(r, 3) & 1) == lax.shift_right_logical(c, 8)
        hidden = jnp.where(own_side, hidden, 0.0).astype(BF16)
        for first in range(0, D, TILE):
            span = slice(first, first + TILE)
            result = dot(hidden, wd[:, span]).astype(BF16)
            back[block, 0, :, span] = result[0:TOK]
            ans[block, 0, :, span] = result[TOK : 2 * TOK]
            inner = first % HALF
            ans2[block, first // HALF, :, inner : inner + TILE] = result[2 * TOK : 3 * TOK]
            ans[block, 1, :, span] = result[3 * TOK :]

    def d_start(block):
        d_copy(block, 0).start()
        d_copy(block, 1).start()
        m_copy(block).wait_recv()
        sum2[block] = (ans2[block, mine].astype(F32) + mate[block].astype(F32)).astype(BF16)
        d_copy(block, 2).start()

    def forward_step(step, carry):
        @pl.when(step < BLOCKS)
        def _():
            block = index_at(step)

            @pl.when(step >= 1)
            def _():
                for side in range(2):
                    a_wait(block, side)

                    @pl.when(a_passed(step, side))
                    def _():
                        a_copy(step, side).start()

            choose(block)
            for kind in (2, 0, 1):
                b_copy(block, kind).start()

        @pl.when((step >= 1) & (step <= BLOCKS))
        def _():
            block = index_at(step - 1)
            b_copy(block, 2).wait_recv()
            f_copy(block).start()

        @pl.when(step >= LAG)
        def _():
            block = index_at(step - LAG)

            @pl.when(step == LAG)
            def _():
                for index in range(4):
                    weight_local(index).wait()
                    weight_remote(index).wait_recv()

            b_copy(block, 0).wait_recv()
            b_copy(block, 1).wait_recv()
            f_wait(block)
            experts(block)
            m_copy(block).start()

        @pl.when(step == BLOCKS + 1)
        def _():
            d_start(mine)

        return carry

    lax.fori_loop(0, BLOCKS + LAG, forward_step, 0)

    def combine(block):
        for kind in range(3):
            d_copy(block, kind).wait_recv()
        info = tok[block, :, :, D:WIDE].reshape(2 * TOK, META)
        code = dot_lanes(info, spread(0))
        r = iota((2 * TOK, rows), 0)
        c = iota((2 * TOK, rows), 1)
        hit = (code == (c & 7).astype(F32)) & ((lax.shift_right_logical(c, 3) & 1) == lax.shift_right_logical(r, 4))
        high = jnp.where(hit, dot_lanes(info, spread(EXPERTS)), 0.0).astype(BF16)
        low = jnp.where(hit, dot_lanes(info, spread(2 * EXPERTS)), 0.0).astype(BF16)
        for first in range(0, D, TILE):
            span = slice(first, first + TILE)
            inner = first % HALF
            answers = jnp.concatenate(
                [
                    back[block, 0, :, span],
                    back[block, 1, :, span],
                    back2[block, first // HALF, :, inner : inner + TILE],
                    back[block, 2, :, span],
                ],
                axis=0,
            )
            total = dot(high, answers) + dot(low, answers)
            acc[0, :, span] = total[0:TOK]
            acc[1, :, span] = total[TOK:]

    def e_copy(position, side):
        block, offset = index_at(position), offset_at(position)
        ahead = lax.rem(position + mine, 2)
        ahead = jnp.where(position == BLOCKS - 1, 1 - side, ahead)
        way = 2 * ahead - 1
        into = jnp.where((position + 1) // 2 == 1, OWN + 1 - ahead, index_of(offset - way, other))
        return remote(
            part.at[block, side], part_in.at[into, side], e_send.at[block, side], e_recv.at[into, side], at(dy=way)
        )

    def e_wait(index, side):
        remote(
            part_in.at[index, side], part_in.at[index, side], e_send.at[0, side], e_recv.at[index, side], right
        ).wait_recv()

    d_start(index_at(BLOCKS - 1))
    d_start(index_at(BLOCKS - 2))

    def backward_step(step, carry):
        position = BLOCKS - 1 - step
        block = index_at(position)
        distance = (position + 1) // 2
        ahead = lax.rem(position + mine, 2)

        @pl.when(position >= 3)
        def _():
            d_start(index_at(position - 2))

        combine(block)
        for side in range(2):
            joined = (distance <= 2) | ((distance == 3) & (ahead == 1 - side))

            @pl.when(joined)
            def _():
                e_wait(block, side)
                part[block, side] = (acc[side] + part_in[block, side].astype(F32)).astype(BF16)

            @pl.when(jnp.logical_not(joined))
            def _():
                part[block, side] = acc[side].astype(BF16)

            e_copy(position, side).start()
        return carry

    lax.fori_loop(0, BLOCKS - 1, backward_step, 0)

    combine(mine)
    first_z, last_z = z == 0, z == NZ - 1

    def z_copy(side):
        return remote(
            fin.at[side], fin_in.at[side], z_send.at[side], z_recv.at[side], at(dz=1 - 2 * side)
        )

    for side, state_ref in enumerate((down_ref, up_ref)):
        e_wait(OWN, side)
        e_wait(OWN + 1, side)
        branch = acc[side] + part_in[OWN, side].astype(F32) + part_in[OWN + 1, side].astype(F32)
        fin[side] = (state_ref[0].astype(F32) + branch).astype(BF16)

        @pl.when(jnp.logical_not(last_z if side == 0 else first_z))
        def _():
            z_copy(side).start()

    @pl.when(first_z)
    def _():
        out_down[0] = fin[1]

    @pl.when(last_z)
    def _():
        out_up[0] = fin[0]

    @pl.when(jnp.logical_not(first_z))
    def _():
        z_copy(0).wait_recv()
        out_down[0] = fin_in[0]

    @pl.when(jnp.logical_not(last_z))
    def _():
        z_copy(1).wait_recv()
        out_up[0] = fin_in[1]

    for side in range(2):
        for way in range(2):
            own_copy(way, side).wait_send()

        @pl.when(jnp.logical_not(last_z if side == 0 else first_z))
        def _():
            z_copy(side).wait_send()

    for index in range(4):
        weight_remote(index).wait_send()

    def drain(position, carry):
        block = index_at(position)
        for kind in range(3):
            b_copy(block, kind).wait_send()
            d_copy(block, kind).wait_send()
        f_copy(block).wait_send()
        m_copy(block).wait_send()
        for side in range(2):

            @pl.when(a_passed(position, side))
            def _():
                a_copy(position, side).wait_send()

            @pl.when(position >= 1)
            def _():
                e_copy(position, side).wait_send()

        return carry

    lax.fori_loop(0, BLOCKS, drain, 0)


def on_device(state_down, state_up, routes, gains, router, w_up, w_down):
    vmem = pl.BlockSpec(memory_space=pltpu.VMEM)
    hbm = pl.BlockSpec(memory_space=pl.ANY)
    dma = pltpu.SemaphoreType.DMA
    return pl.pallas_call(
        kernel,
        out_shape=(
            jax.ShapeDtypeStruct(state_down.shape, BF16),
            jax.ShapeDtypeStruct(state_up.shape, BF16),
        ),
        in_specs=[vmem] * 5 + [hbm] * 2,
        out_specs=(vmem, vmem),
        scratch_shapes=[
            pltpu.VMEM((BLOCKS, 2, TOK, WIDE), BF16),
            pltpu.VMEM((BLOCKS, 2, TOK, D), BF16),
            pltpu.VMEM((BLOCKS, 2, TOK, HALF), BF16),
            pltpu.VMEM((BLOCKS, 3, TOK, D), BF16),
            pltpu.VMEM((BLOCKS, 2, TOK, HALF), BF16),
            pltpu.VMEM((BLOCKS, 2, TOK, D), BF16),
            pltpu.VMEM((BLOCKS, 2, TOK, HALF), BF16),
            pltpu.VMEM((BLOCKS, TOK, HALF), BF16),
            pltpu.VMEM((BLOCKS, TOK, HALF), BF16),
            pltpu.VMEM((BLOCKS, 3, TOK, D), BF16),
            pltpu.VMEM((BLOCKS, 2, TOK, HALF), BF16),
            pltpu.VMEM((BLOCKS, 2, TOK, D), BF16),
            pltpu.VMEM((BLOCKS + 2, 2, TOK, D), BF16),
            pltpu.VMEM((2, TOK, D), F32),
            pltpu.VMEM((D, 4 * HID), BF16),
            pltpu.VMEM((4 * HID, D), BF16),
            pltpu.VMEM((2, TOK, D), BF16),
            pltpu.VMEM((2, TOK, D), BF16),
            dma((2, 2)),
            dma((BLOCKS, 2)),
            dma((BLOCKS, 2)),
            dma((BLOCKS, 3)),
            dma((BLOCKS, 3)),
            dma((BLOCKS,)),
            dma((BLOCKS,)),
            dma((BLOCKS,)),
            dma((BLOCKS,)),
            dma((BLOCKS, 3)),
            dma((BLOCKS, 3)),
            dma((BLOCKS, 2)),
            dma((BLOCKS + 2, 2)),
            dma((4,)),
            dma((4,)),
            dma((4,)),
            dma((2,)),
            dma((2,)),
        ],
        compiler_params=pltpu.CompilerParams(
            collective_id=0, has_side_effects=True, vmem_limit_bytes=56 * 2**20
        ),
        name="routed_experts",
    )(state_down, state_up, routes[0, 0], gains, jnp.swapaxes(router[0], 1, 2), w_up, w_down)


def solution(mesh):
    in_specs = (
        P("pipe", "expert", None),
        P("pipe", "expert", None),
        P(None, "pipe", None, "expert", None),
        P("pipe", None, None),
        P("pipe", None, None, None),
        P("pipe", None, None, "expert"),
        P("pipe", None, "expert", None),
    )
    out_specs = (P("pipe", "expert", None), P("pipe", "expert", None))
    return jax.shard_map(
        on_device, mesh=mesh, in_specs=in_specs, out_specs=out_specs, check_vma=False
    )
```

time: 392 us -> 99.9 us (0.25)
  the two profiles are of different devices: /device:TPU:259 before, /device:TPU:64 now
where the time goes in v1:
time: 99.9 us; the launch traced here: 99.7 us
  Pallas kernels  94.6 us (95%)
  local copies, waits for them, and re-layouts  4.47 us (4%)
    pallas_call x1, Pallas kernels, on_device(): pl.pallas_call(kernel, out_shape=(jax.ShapeDtypeStruct(state_down.shape,...  94.6 us
    unnamed x2, local copies, waits for them, and re-layouts  3.1 us

profile of v1, /device:TPU:64, one launch (start us, length us, event | category | flops | bytes accessed | tf_op | source)
XLA Modules:
  0.0 99.7 jit_solution(8869060151642609631)
XLA Ops:
  0.6 1.4 %copy.9.routes_ref = s32[2,16,2]{2,1,0:T(8,128)} copy(s32[2,16,2]{1,2,0:T(2,128)} %bitcast.5) | data formatting | bytes 512 | tf_op jit(solution)/shard_map/squeeze | solution.py:488
  2.0 94.6 %routed_experts.1 = (bf16[1,16,3584]{2,1,0:T(8,128)(2,1)}, bf16[1,16,3584]{2,1,0:T(8,128)(2,1)}) custom-call(bf16[1,16,3584]{2,1,0:T(8,128)(2,1)} %down_ref.1, bf16[1,16,3584]{2,1,0:T(8,128)(2,1)} %up_ref.1, s32[2,16,2]{2,1,0:T(8,128)} %copy.9.routes_ref, f32[1,2,3584]{2,1,0:T(2,128)} %gains_ref.1, bf16[2,8,3584]{2,1,0:T(8,128)(2,1)} %bitcast.4, ...), custom_call_target="tpu_custom_call" | custom-call | tf_op jit(solution)/shard_map/routed_experts/pallas_call | solution.py:438
  96.6 1.6 %copy.12 = bf16[1,16,3584]{2,1,0:T(8,128)(2,1)} copy(bf16[1,16,3584]{2,1,0:T(8,128)(2,1)} %get-tuple-element.4) | data formatting | bytes 229376
  98.1 1.6 %copy.13 = bf16[1,16,3584]{2,1,0:T(8,128)(2,1)} copy(bf16[1,16,3584]{2,1,0:T(8,128)(2,1)} %get-tuple-element.5) | data formatting | bytes 229376

commit v2 on v1

v2 whole, which is shorter than its diff:
```python
import functools

import jax
import jax.numpy as jnp
from jax import lax
from jax.experimental import pallas as pl
from jax.experimental.pallas import tpu as pltpu
from jax.sharding import PartitionSpec as P

MESH = pl.DeviceIdType.MESH
EPSILON = 1e-06
ROUTE_SCALE = 2.5

NX, NY, NZ = 4, 8, 8
EXPERTS = 8
TOK = 16
CAP = 8
D = 3584
HALF = D // 2
META = 128
WIDE = HALF + META
TILE = 256
HID = 128
BLOCKS = NY
OWN = BLOCKS
LAG_PASS = 2
LAG = 5
FILLER = 3

F32 = jnp.float32
BF16 = jnp.bfloat16


def dot(a, b):
    return jnp.dot(a, b, preferred_element_type=F32)


def dot_lanes(a, b):
    return lax.dot_general(a, b, (((1,), (1,)), ((), ())), preferred_element_type=F32)


def iota(shape, axis):
    return lax.broadcasted_iota(jnp.int32, shape, axis)


def kernel(
    down_ref, up_ref, routes_ref, gains_ref, router_ref, w_up_ref, w_down_ref,
    out_down, out_up,
    tok, sel, sel2, got, got2, ans, ans2, mate, sum2, back, back2, part, part_in, acc, wu, wd, fin, fin_in,
    own_send, a_send, a_recv, b_send, b_recv, f_send, f_recv, m_send, m_recv, d_send, d_recv,
    e_send, e_recv, w_local, w_send, w_recv, z_send, z_recv,
):
    z = lax.axis_index("pipe")
    place = lax.axis_index("expert")
    x = place // (2 * NY)
    y = lax.rem(place // 2, NY)
    core = lax.rem(place, 2)
    half_of_experts = y // (NY // 2)
    mine = lax.rem(y, 2)
    other = 1 - mine

    def at(dz=0, dx=0, dy=0):
        xx = lax.rem(x + dx + NX, NX)
        yy = lax.rem(y + dy + NY, NY)
        return (lax.rem(z + dz + NZ, NZ), (xx * NY + yy) * 2 + core)

    sibling = (z, place + 1 - 2 * core)
    pair = (z, place + 2 - 4 * mine)
    right, left = at(dy=1), at(dy=-1)

    def index_of(offset, parity):
        o = lax.rem(offset + parity + 2 * NY, NY)
        return jnp.where(o == 0, 0, jnp.where(o <= NY // 2, 2 * o - 1, 2 * (NY - o)))

    def index_at(position):
        return position + mine * (1 - 2 * lax.rem(position, 2))

    def offset_at(position):
        ahead = lax.rem(position + mine, 2)
        return (2 * ahead - 1) * ((position + 1) // 2)

    barrier = pltpu.get_barrier_semaphore()
    friends = (right, left, at(dx=1), at(dx=-1), at(dx=2), sibling, at(dz=1), at(dz=-1))
    for friend in friends:
        pl.semaphore_signal(barrier, inc=1, device_id=friend, device_id_type=MESH)

    def remote(src, dst, send, recv, device):
        return pltpu.make_async_remote_copy(
            src_ref=src, dst_ref=dst, send_sem=send, recv_sem=recv, device_id=device, device_id_type=MESH
        )

    def weight_views(index):
        side = index // 2
        if index % 2 == 0:
            return w_up_ref.at[0, side], [wu.at[:, pl.ds((2 * side + o) * HID, HID)] for o in (0, 1)]
        return w_down_ref.at[0, side], [wd.at[pl.ds((2 * side + o) * HID, HID), :] for o in (0, 1)]

    def weight_local(index):
        src, views = weight_views(index)
        return pltpu.make_async_copy(src, views[0], w_local.at[index])

    def weight_remote(index):
        src, views = weight_views(index)
        return remote(src, views[1], w_send.at[index], w_recv.at[index], sibling)

    for index in range(4):
        weight_local(index).start()

    eye = (iota((TOK, TOK), 1) == iota((TOK, TOK), 0)).astype(BF16)
    earlier = (iota((TOK, TOK), 1) < iota((TOK, TOK), 0)).astype(BF16)

    def put(first):
        return (iota((EXPERTS, META), 1) == iota((EXPERTS, META), 0) + first).astype(BF16)

    for side, state_ref in enumerate((down_ref, up_ref)):
        wide = state_ref[0].astype(F32)
        scale_rows = lax.rsqrt(jnp.mean(wide * wide, axis=-1, keepdims=True) + EPSILON)
        normed = (wide * scale_rows * gains_ref[0, side : side + 1, :]).astype(BF16)
        own_rows = slice(side * TOK, (side + 1) * TOK)
        for half in range(2):
            tok[mine, half, own_rows, 0:HALF] = normed[:, half * HALF : (half + 1) * HALF]
        logits = dot_lanes(normed, router_ref[side])
        picked = routes_ref[side]
        named = iota((EXPERTS, TOK), 0)
        hit_rows = ((picked[0:1, :] == named) | (picked[1:2, :] == named)).astype(F32).astype(BF16)
        hit = dot_lanes(eye, hit_rows)
        slot = dot_lanes(earlier, hit_rows)
        affinity = hit * jax.nn.sigmoid(logits)
        weight = ROUTE_SCALE * affinity / jnp.sum(affinity, axis=-1, keepdims=True)
        code = jnp.where(hit > 0.5, slot, -1.0).astype(BF16)
        high = weight.astype(BF16)
        low = (weight - high.astype(F32)).astype(BF16)
        info = dot(code, put(0)) + dot(high, put(EXPERTS)) + dot(low, put(2 * EXPERTS))
        tok[mine, 0, own_rows, HALF:WIDE] = info.astype(BF16)

    pl.semaphore_wait(barrier, len(friends))

    def tok_at(block, half):
        return tok.at[block, half] if half == 0 else tok.at[block, half, :, 0:HALF]

    def own_copy(way, half):
        into = index_of(1 - 2 * way, other)
        return remote(
            tok_at(mine, half), tok_at(into, half), own_send.at[way, half], a_recv.at[into, half],
            right if way else left,
        )

    for half in range(2):
        for way in range(2):
            own_copy(way, half).start()
    for index in range(4):
        weight_remote(index).start()

    zeros_half = jnp.zeros((TOK, HALF), BF16)
    for block in range(BLOCKS):
        back2[block, other] = zeros_half

    rows = 4 * TOK
    row = iota((rows, META), 0)
    expert_of_row = 2 * lax.rem(x + lax.shift_right_logical(row, 4), NX) + half_of_experts
    lane = iota((rows, META), 1)

    def spread(first):
        return (lane == expert_of_row + first).astype(BF16)

    def a_passed(position, half):
        ahead = lax.rem(position + mine, 2)
        last = 2 + (ahead if half else 1 - ahead)
        return (position >= 1) & ((position + 1) // 2 <= last)

    def a_copy(position, half):
        block, offset = index_at(position), offset_at(position)
        way = 1 - 2 * lax.rem(position + mine, 2)
        into = index_of(offset - way, other)
        return remote(
            tok_at(block, half), tok_at(into, half), a_send.at[block, half], a_recv.at[into, half], at(dy=way)
        )

    def a_wait(block, half):
        remote(
            tok_at(block, half), tok_at(block, half), a_send.at[block, half], a_recv.at[block, half], right
        ).wait_recv()

    def b_copy(block, kind, half=0):
        if kind == 2:
            src, dst, number = sel2.at[block, mine], got2.at[block, mine], 4
        else:
            src, dst, number = sel.at[block, kind, half], got.at[block, 1 + kind, half], 2 * kind + half
        return remote(src, dst, b_send.at[block, number], b_recv.at[block, number], at(dx=(1, -1, 2)[kind]))

    def f_copy(block):
        return remote(got2.at[block, mine], got2.at[block, mine], f_send.at[block], f_recv.at[block], pair)

    def f_wait(block):
        remote(
            got2.at[block, other], got2.at[block, other], f_send.at[block], f_recv.at[block], pair
        ).wait_recv()

    def m_copy(block):
        return remote(ans2.at[block, other], mate.at[block], m_send.at[block], m_recv.at[block], pair)

    def d_copy(block, kind, half=0):
        if kind == 2:
            src, dst, number = sum2.at[block], back2.at[block, mine], 4
        else:
            src, dst, number = ans.at[block, kind, half], back.at[block, 1 + kind, half], 2 * kind + half
        return remote(src, dst, d_send.at[block, number], d_recv.at[block, number], at(dx=(-1, 1, 2)[kind]))

    def choose(block, half):
        info = tok[block, 0, :, HALF:WIDE]
        code = dot_lanes(spread(0), info)
        r = iota((rows, 2 * TOK), 0)
        c = iota((rows, 2 * TOK), 1)
        hit = (code == (r & 7).astype(F32)) & ((lax.shift_right_logical(r, 3) & 1) == lax.shift_right_logical(c, 4))
        table = hit.astype(F32).astype(BF16)
        for first in range(0, HALF, TILE):
            span = slice(first, first + TILE)
            picked = dot(table, tok[block, half, :, span]).astype(BF16)
            got[block, 0, half, :, span] = picked[0:TOK]
            sel[block, 0, half, :, span] = picked[TOK : 2 * TOK]
            sel2[block, half, :, span] = picked[2 * TOK : 3 * TOK]
            sel[block, 1, half, :, span] = picked[3 * TOK :]

    def experts(block):
        total = jnp.zeros((rows, 4 * HID), F32)
        for half in range(2):
            lhs = jnp.concatenate(
                [got[block, 0, half], got[block, 1, half], got2[block, half], got[block, 2, half]], axis=0
            )
            total = total + dot(lhs, wu[half * HALF : (half + 1) * HALF, :])
        hidden = total * jax.nn.sigmoid(total)
        r = iota((rows, 4 * HID), 0)
        c = iota((rows, 4 * HID), 1)
        own_side = (lax.shift_right_logical(r, 3) & 1) == lax.shift_right_logical(c, 8)
        hidden = jnp.where(own_side, hidden, 0.0).astype(BF16)
        for half in range(2):
            for first in range(0, HALF, TILE):
                span = slice(first, first + TILE)
                result = dot(hidden, wd[:, half * HALF + first : half * HALF + first + TILE]).astype(BF16)
                back[block, 0, half, :, span] = result[0:TOK]
                ans[block, 0, half, :, span] = result[TOK : 2 * TOK]
                ans2[block, half, :, span] = result[2 * TOK : 3 * TOK]
                ans[block, 1, half, :, span] = result[3 * TOK :]

    def d_near(block, half):
        for kind in range(2):
            d_copy(block, kind, half).start()

    def d_far(block):
        m_copy(block).wait_recv()
        sum2[block] = (ans2[block, mine].astype(F32) + mate[block].astype(F32)).astype(BF16)
        d_copy(block, 2).start()

    def d_whole(block):
        d_near(block, 0)
        d_near(block, 1)
        d_far(block)

    def forward_step(step, carry):
        @pl.when(step < BLOCKS)
        def _():
            block = index_at(step)
            for half in range(2):

                @pl.when(step >= 1)
                def _():
                    a_wait(block, half)

                    @pl.when(a_passed(step, half))
                    def _():
                        a_copy(step, half).start()

                choose(block, half)

                @pl.when(mine == half)
                def _():
                    b_copy(block, 2).start()

                for kind in range(2):
                    b_copy(block, kind, half).start()

        @pl.when((step >= LAG_PASS) & (step < BLOCKS + LAG_PASS))
        def _():
            block = index_at(step - LAG_PASS)
            b_copy(block, 2).wait_recv()
            f_copy(block).start()

        @pl.when(step >= LAG)
        def _():
            block = index_at(step - LAG)

            @pl.when(step == LAG)
            def _():
                for index in range(4):
                    weight_local(index).wait()
                    weight_remote(index).wait_recv()

            for half in range(2):
                for kind in range(2):
                    b_copy(block, kind, half).wait_recv()
            f_wait(block)
            experts(block)
            m_copy(block).start()

            @pl.when(step >= BLOCKS + LAG - 2)
            def _():
                d_near(block, 0)
                d_near(block, 1)

        @pl.when(step == BLOCKS)
        def _():
            d_whole(index_at(FILLER))

        return carry

    lax.fori_loop(0, BLOCKS + LAG, forward_step, 0)

    def combine(block, half):
        for kind in range(2):
            d_copy(block, kind, half).wait_recv()

        @pl.when(mine == half)
        def _():
            d_copy(block, 2).wait_recv()

        info = tok[block, 0, :, HALF:WIDE]
        code = dot_lanes(info, spread(0))
        r = iota((2 * TOK, rows), 0)
        c = iota((2 * TOK, rows), 1)
        hit = (code == (c & 7).astype(F32)) & ((lax.shift_right_logical(c, 3) & 1) == lax.shift_right_logical(r, 4))
        high = jnp.where(hit, dot_lanes(info, spread(EXPERTS)), 0.0).astype(BF16)
        low = jnp.where(hit, dot_lanes(info, spread(2 * EXPERTS)), 0.0).astype(BF16)
        for first in range(0, HALF, TILE):
            span = slice(first, first + TILE)
            answers = jnp.concatenate(
                [
                    back[block, 0, half, :, span],
                    back[block, 1, half, :, span],
                    back2[block, half, :, span],
                    back[block, 2, half, :, span],
                ],
                axis=0,
            )
            acc[half, :, span] = dot(high, answers) + dot(low, answers)

    def e_copy(position, half):
        block, offset = index_at(position), offset_at(position)
        ahead = lax.rem(position + mine, 2)
        ahead = jnp.where(position == BLOCKS - 1, 1 - half, ahead)
        way = 2 * ahead - 1
        into = jnp.where((position + 1) // 2 == 1, OWN + 1 - ahead, index_of(offset - way, other))
        return remote(
            part.at[block, half], part_in.at[into, half], e_send.at[block, half], e_recv.at[into, half], at(dy=way)
        )

    def e_wait(index, half):
        remote(
            part_in.at[index, half], part_in.at[index, half], e_send.at[0, half], e_recv.at[index, half], right
        ).wait_recv()

    def join(position, half):
        block = index_at(position)
        distance = (position + 1) // 2
        ahead = lax.rem(position + mine, 2)
        combine(block, half)
        joined = (distance <= 2) | ((distance == 3) & (ahead == 1 - half))

        @pl.when(joined)
        def _():
            e_wait(block, half)
            part[block, half] = (acc[half] + part_in[block, half].astype(F32)).astype(BF16)

        @pl.when(jnp.logical_not(joined))
        def _():
            part[block, half] = acc[half].astype(BF16)

        e_copy(position, half).start()

    d_far(index_at(BLOCKS - 1))
    d_far(index_at(BLOCKS - 2))
    for position in range(BLOCKS - 3, -1, -1):
        if position != FILLER:
            d_whole(index_at(position))
    for half in range(2):
        join(BLOCKS - 1, half)

    def backward_step(step, carry):
        distance = NY // 2 - 1 - step

        for half in range(2):
            join(2 * distance, half)
            join(2 * distance - 1, half)

        return carry

    lax.fori_loop(0, NY // 2 - 1, backward_step, 0)

    first_z, last_z = z == 0, z == NZ - 1

    def z_copy(side, half):
        return remote(
            fin.at[side, half], fin_in.at[side, half], z_send.at[side, half], z_recv.at[side, half],
            at(dz=1 - 2 * side),
        )

    for half in range(2):
        combine(mine, half)
        span = slice(half * HALF, (half + 1) * HALF)
        e_wait(OWN, half)
        e_wait(OWN + 1, half)
        for side, state_ref in enumerate((down_ref, up_ref)):
            own_rows = slice(side * TOK, (side + 1) * TOK)
            branch = acc[half, own_rows] + part_in[OWN, half, own_rows].astype(F32)
            branch = branch + part_in[OWN + 1, half, own_rows].astype(F32)
            fin[side, half] = (state_ref[0, :, span].astype(F32) + branch).astype(BF16)

            @pl.when(jnp.logical_not(last_z if side == 0 else first_z))
            def _():
                z_copy(side, half).start()

    for half in range(2):
        for way in range(2):
            own_copy(way, half).wait_send()

    for index in range(4):
        weight_remote(index).wait_send()

    def drain(position, carry):
        block = index_at(position)
        for half in range(2):
            for kind in range(2):
                b_copy(block, kind, half).wait_send()
                d_copy(block, kind, half).wait_send()

            @pl.when(a_passed(position, half))
            def _():
                a_copy(position, half).wait_send()

            @pl.when(position >= 1)
            def _():
                e_copy(position, half).wait_send()

        b_copy(block, 2).wait_send()
        d_copy(block, 2).wait_send()
        f_copy(block).wait_send()
        m_copy(block).wait_send()
        return carry

    lax.fori_loop(0, BLOCKS, drain, 0)

    for half in range(2):
        span = slice(half * HALF, (half + 1) * HALF)

        @pl.when(first_z)
        def _():
            out_down[0, :, span] = fin[1, half]

        @pl.when(last_z)
        def _():
            out_up[0, :, span] = fin[0, half]

        @pl.when(jnp.logical_not(first_z))
        def _():
            z_copy(0, half).wait_recv()
            out_down[0, :, span] = fin_in[0, half]
            z_copy(1, half).wait_send()

        @pl.when(jnp.logical_not(last_z))
        def _():
            z_copy(1, half).wait_recv()
            out_up[0, :, span] = fin_in[1, half]
            z_copy(0, half).wait_send()


def on_device(state_down, state_up, routes, gains, router, w_up, w_down):
    vmem = pl.BlockSpec(memory_space=pltpu.VMEM)
    hbm = pl.BlockSpec(memory_space=pl.ANY)
    dma = pltpu.SemaphoreType.DMA
    return pl.pallas_call(
        kernel,
        out_shape=(
            jax.ShapeDtypeStruct(state_down.shape, BF16),
            jax.ShapeDtypeStruct(state_up.shape, BF16),
        ),
        in_specs=[vmem] * 5 + [hbm] * 2,
        out_specs=(vmem, vmem),
        scratch_shapes=[
            pltpu.VMEM((BLOCKS, 2, 2 * TOK, WIDE), BF16),
            pltpu.VMEM((BLOCKS, 2, 2, TOK, HALF), BF16),
            pltpu.VMEM((BLOCKS, 2, TOK, HALF), BF16),
            pltpu.VMEM((BLOCKS, 3, 2, TOK, HALF), BF16),
            pltpu.VMEM((BLOCKS, 2, TOK, HALF), BF16),
            pltpu.VMEM((BLOCKS, 2, 2, TOK, HALF), BF16),
            pltpu.VMEM((BLOCKS, 2, TOK, HALF), BF16),
            pltpu.VMEM((BLOCKS, TOK, HALF), BF16),
            pltpu.VMEM((BLOCKS, TOK, HALF), BF16),
            pltpu.VMEM((BLOCKS, 3, 2, TOK, HALF), BF16),
            pltpu.VMEM((BLOCKS, 2, TOK, HALF), BF16),
            pltpu.VMEM((BLOCKS, 2, 2 * TOK, HALF), BF16),
            pltpu.VMEM((BLOCKS + 2, 2, 2 * TOK, HALF), BF16),
            pltpu.VMEM((2, 2 * TOK, HALF), F32),
            pltpu.VMEM((D, 4 * HID), BF16),
            pltpu.VMEM((4 * HID, D), BF16),
            pltpu.VMEM((2, 2, TOK, HALF), BF16),
            pltpu.VMEM((2, 2, TOK, HALF), BF16),
            dma((2, 2)),
            dma((BLOCKS, 2)),
            dma((BLOCKS, 2)),
            dma((BLOCKS, 5)),
            dma((BLOCKS, 5)),
            dma((BLOCKS,)),
            dma((BLOCKS,)),
            dma((BLOCKS,)),
            dma((BLOCKS,)),
            dma((BLOCKS, 5)),
            dma((BLOCKS, 5)),
            dma((BLOCKS, 2)),
            dma((BLOCKS + 2, 2)),
            dma((4,)),
            dma((4,)),
            dma((4,)),
            dma((2, 2)),
            dma((2, 2)),
        ],
        compiler_params=pltpu.CompilerParams(
            collective_id=0, has_side_effects=True, vmem_limit_bytes=56 * 2**20
        ),
        name="routed_experts",
    )(state_down, state_up, jnp.swapaxes(routes[0, 0], 1, 2), gains, jnp.swapaxes(router[0], 1, 2), w_up, w_down)


def solution(mesh):
    in_specs = (
        P("pipe", "expert", None),
        P("pipe", "expert", None),
        P(None, "pipe", None, "expert", None),
        P("pipe", None, None),
        P("pipe", None, None, None),
        P("pipe", None, None, "expert"),
        P("pipe", None, "expert", None),
    )
    out_specs = (P("pipe", "expert", None), P("pipe", "expert", None))
    return jax.shard_map(
        on_device, mesh=mesh, in_specs=in_specs, out_specs=out_specs, check_vma=False
    )
```

time: 99.9 us -> 93.6 us (0.937)
  the two profiles are of different devices: /device:TPU:64 before, /device:TPU:8 now
where the time goes in v2:
time: 93.6 us; the launch traced here: 93.4 us
  Pallas kernels  89.7 us (96%)
  local copies, waits for them, and re-layouts  3.1 us (3%)
    pallas_call x1, Pallas kernels, on_device(): pl.pallas_call(kernel, out_shape=(jax.ShapeDtypeStruct(state_down.shape,...  89.7 us
    unnamed x2, local copies, waits for them, and re-layouts  3.1 us

profile of v2, /device:TPU:8, one launch (start us, length us, event | category | flops | bytes accessed | tf_op | source)
XLA Modules:
  0.0 93.4 jit_solution(12041247781103439300)
XLA Ops:
  0.6 89.7 %routed_experts.1 = (bf16[1,16,3584]{2,1,0:T(8,128)(2,1)}, bf16[1,16,3584]{2,1,0:T(8,128)(2,1)}) custom-call(bf16[1,16,3584]{2,1,0:T(8,128)(2,1)} %down_ref.1, bf16[1,16,3584]{2,1,0:T(8,128)(2,1)} %up_ref.1, s32[2,2,16]{2,1,0:T(2,128)} %bitcast.7, f32[1,2,3584]{2,1,0:T(2,128)} %gains_ref.1, bf16[2,8,3584]{2,1,0:T(8,128)(2,1)} %bitcast.6, ...), custom_call_target="tpu_custom_call" | custom-call | tf_op jit(solution)/shard_map/routed_experts/pallas_call | solution.py:479
  90.3 1.6 %copy.11 = bf16[1,16,3584]{2,1,0:T(8,128)(2,1)} copy(bf16[1,16,3584]{2,1,0:T(8,128)(2,1)} %get-tuple-element.4) | data formatting | bytes 229376
  91.9 1.6 %copy.12 = bf16[1,16,3584]{2,1,0:T(8,128)(2,1)} copy(bf16[1,16,3584]{2,1,0:T(8,128)(2,1)} %get-tuple-element.5) | data formatting | bytes 229376

commit v3 on v2

--- a/solution.py
+++ b/solution.py
@@ -22,7 +22,6 @@
 TILE = 256
 HID = 128
 BLOCKS = NY
-OWN = BLOCKS
 LAG_PASS = 2
 LAG = 5
 FILLER = 3
@@ -48,7 +47,7 @@
     out_down, out_up,
     tok, sel, sel2, got, got2, ans, ans2, mate, sum2, back, back2, part, part_in, acc, wu, wd, fin, fin_in,
     own_send, a_send, a_recv, b_send, b_recv, f_send, f_recv, m_send, m_recv, d_send, d_recv,
-    e_send, e_recv, w_local, w_send, w_recv, z_send, z_recv,
+    e_send, e_recv, l_send, w_local, w_send, w_recv, z_send, z_recv,
 ):
     z = lax.axis_index("pipe")
     place = lax.axis_index("expert")
@@ -80,7 +79,8 @@
         return (2 * ahead - 1) * ((position + 1) // 2)
 
     barrier = pltpu.get_barrier_semaphore()
-    friends = (right, left, at(dx=1), at(dx=-1), at(dx=2), sibling, at(dz=1), at(dz=-1))
+    friends = (right, left, at(dx=1), at(dx=-1), at(dx=2), sibling)
+    friends += tuple(at(dz=dz, dy=dy) for dz in (1, -1) for dy in (0, 1, -1))
     for friend in friends:
         pl.semaphore_signal(barrier, inc=1, device_id=friend, device_id_type=MESH)
 
@@ -348,7 +348,7 @@
         ahead = lax.rem(position + mine, 2)
         ahead = jnp.where(position == BLOCKS - 1, 1 - half, ahead)
         way = 2 * ahead - 1
-        into = jnp.where((position + 1) // 2 == 1, OWN + 1 - ahead, index_of(offset - way, other))
+        into = index_of(offset - way, other)
         return remote(
             part.at[block, half], part_in.at[into, half], e_send.at[block, half], e_recv.at[into, half], at(dy=way)
         )
@@ -374,7 +374,26 @@
         def _():
             part[block, half] = acc[half].astype(BF16)
 
-        e_copy(position, half).start()
+    first_z, last_z = z == 0, z == NZ - 1
+    stays = (last_z, first_z)
+    steps_z = (jnp.where(last_z, 0, 1), jnp.where(first_z, 0, -1))
+    results = (jnp.where(last_z, 1, 0), jnp.where(first_z, 0, 1))
+
+    def last_copy(position, half, side):
+        block = index_at(position)
+        ahead = lax.rem(position + mine, 2)
+        result, source = results[side], 2 - ahead
+        return remote(
+            part.at[block, half, pl.ds(side * TOK, TOK)], fin_in.at[result, source, half],
+            l_send.at[position, half, side], z_recv.at[result, source, half],
+            at(dz=steps_z[side], dy=2 * ahead - 1),
+        )
+
+    def z_copy(side, half):
+        return remote(
+            fin.at[side, half], fin_in.at[side, 0, half], z_send.at[side, half], z_recv.at[side, 0, half],
+            at(dz=1 - 2 * side),
+        )
 
     d_far(index_at(BLOCKS - 1))
     d_far(index_at(BLOCKS - 2))
@@ -383,40 +402,41 @@
             d_whole(index_at(position))
     for half in range(2):
         join(BLOCKS - 1, half)
+        e_copy(BLOCKS - 1, half).start()
 
     def backward_step(step, carry):
         distance = NY // 2 - 1 - step
 
         for half in range(2):
-            join(2 * distance, half)
-            join(2 * distance - 1, half)
+            for position in (2 * distance, 2 * distance - 1):
+                join(position, half)
+                e_copy(position, half).start()
 
         return carry
 
-    lax.fori_loop(0, NY // 2 - 1, backward_step, 0)
-
-    first_z, last_z = z == 0, z == NZ - 1
-
-    def z_copy(side, half):
-        return remote(
-            fin.at[side, half], fin_in.at[side, half], z_send.at[side, half], z_recv.at[side, half],
-            at(dz=1 - 2 * side),
-        )
+    lax.fori_loop(0, NY // 2 - 2, backward_step, 0)
+
+    for half in range(2):
+        for position in (2, 1):
+            join(position, half)
+            for side in range(2):
+                last_copy(position, half, side).start()
 
     for half in range(2):
         combine(mine, half)
         span = slice(half * HALF, (half + 1) * HALF)
-        e_wait(OWN, half)
-        e_wait(OWN + 1, half)
         for side, state_ref in enumerate((down_ref, up_ref)):
-            own_rows = slice(side * TOK, (side + 1) * TOK)
-            branch = acc[half, own_rows] + part_in[OWN, half, own_rows].astype(F32)
-            branch = branch + part_in[OWN + 1, half, own_rows].astype(F32)
-            fin[side, half] = (state_ref[0, :, span].astype(F32) + branch).astype(BF16)
-
-            @pl.when(jnp.logical_not(last_z if side == 0 else first_z))
+            fin[side, half] = (
+                state_ref[0, :, span].astype(F32) + acc[half, side * TOK : (side + 1) * TOK]
+            ).astype(BF16)
+
+            @pl.when(jnp.logical_not(stays[side]))
             def _():
                 z_copy(side, half).start()
+
+            @pl.when(stays[side])
+            def _():
+                fin_in[1 - side, 0, half] = fin[side, half]
 
     for half in range(2):
         for way in range(2):
@@ -436,7 +456,7 @@
             def _():
                 a_copy(position, half).wait_send()
 
-            @pl.when(position >= 1)
+            @pl.when(position >= 3)
             def _():
                 e_copy(position, half).wait_send()
 
@@ -449,27 +469,28 @@
     lax.fori_loop(0, BLOCKS, drain, 0)
 
     for half in range(2):
+        for position in (2, 1):
+            for side in range(2):
+                last_copy(position, half, side).wait_send()
         span = slice(half * HALF, (half + 1) * HALF)
-
-        @pl.when(first_z)
-        def _():
-            out_down[0, :, span] = fin[1, half]
-
-        @pl.when(last_z)
-        def _():
-            out_up[0, :, span] = fin[0, half]
-
-        @pl.when(jnp.logical_not(first_z))
-        def _():
-            z_copy(0, half).wait_recv()
-            out_down[0, :, span] = fin_in[0, half]
-            z_copy(1, half).wait_send()
-
-        @pl.when(jnp.logical_not(last_z))
-        def _():
-            z_copy(1, half).wait_recv()
-            out_up[0, :, span] = fin_in[1, half]
-            z_copy(0, half).wait_send()
+        for side, out in enumerate((out_down, out_up)):
+
+            @pl.when(jnp.logical_not(stays[side]))
+            def _():
+                z_copy(side, half).wait_send()
+
+            @pl.when(jnp.logical_not(stays[1 - side]))
+            def _():
+                z_copy(side, half).wait_recv()
+
+            total = fin_in[side, 0, half].astype(F32)
+            for source in (1, 2):
+                remote(
+                    fin_in.at[side, source, half], fin_in.at[side, source, half],
+                    z_send.at[side, half], z_recv.at[side, source, half], right,
+                ).wait_recv()
+                total = total + fin_in[side, source, half].astype(F32)
+            out[0, :, span] = total.astype(BF16)
 
 
 def on_device(state_down, state_up, routes, gains, router, w_up, w_down):
@@ -479,8 +500,8 @@
     return pl.pallas_call(
         kernel,
         out_shape=(
-            jax.ShapeDtypeStruct(state_down.shape, BF16),
-            jax.ShapeDtypeStruct(state_up.shape, BF16),
+            pltpu.VMEM(state_down.shape, BF16),
+            pltpu.VMEM(state_up.shape, BF16),
         ),
         in_specs=[vmem] * 5 + [hbm] * 2,
         out_specs=(vmem, vmem),
@@ -497,12 +518,12 @@
             pltpu.VMEM((BLOCKS, 3, 2, TOK, HALF), BF16),
             pltpu.VMEM((BLOCKS, 2, TOK, HALF), BF16),
             pltpu.VMEM((BLOCKS, 2, 2 * TOK, HALF), BF16),
-            pltpu.VMEM((BLOCKS + 2, 2, 2 * TOK, HALF), BF16),
+            pltpu.VMEM((BLOCKS, 2, 2 * TOK, HALF), BF16),
             pltpu.VMEM((2, 2 * TOK, HALF), F32),
             pltpu.VMEM((D, 4 * HID), BF16),
             pltpu.VMEM((4 * HID, D), BF16),
             pltpu.VMEM((2, 2, TOK, HALF), BF16),
-            pltpu.VMEM((2, 2, TOK, HALF), BF16),
+            pltpu.VMEM((2, 3, 2, TOK, HALF), BF16),
             dma((2, 2)),
             dma((BLOCKS, 2)),
             dma((BLOCKS, 2)),
@@ -515,12 +536,13 @@
             dma((BLOCKS, 5)),
             dma((BLOCKS, 5)),
             dma((BLOCKS, 2)),
-            dma((BLOCKS + 2, 2)),
+            dma((BLOCKS, 2)),
+            dma((3, 2, 2)),
             dma((4,)),
             dma((4,)),
             dma((4,)),
             dma((2, 2)),
-            dma((2, 2)),
+            dma((2, 3, 2)),
         ],
         compiler_params=pltpu.CompilerParams(
             collective_id=0, has_side_effects=True, vmem_limit_bytes=56 * 2**20

time: 93.6 us -> 90.1 us (0.963)
  the two profiles are of different devices: /device:TPU:8 before, /device:TPU:64 now
where the time goes in v3:
time: 90.1 us; the launch traced here: 89.9 us
  Pallas kernels  88 us (98%)
  local copies, waits for them, and re-layouts  1.29 us (1%)
    pallas_call x1, Pallas kernels, on_device(): pl.pallas_call(kernel, out_shape=(pltpu.VMEM(state_down.shape, BF16), plt...  88 us

profile of v3, /device:TPU:64, one launch (start us, length us, event | category | flops | bytes accessed | tf_op | source)
XLA Modules:
  0.0 89.9 jit_solution(16625816927931281819)
XLA Ops:
  0.6 88.0 %routed_experts.1 = (bf16[1,16,3584]{2,1,0:T(8,128)(2,1)S(1)}, bf16[1,16,3584]{2,1,0:T(8,128)(2,1)S(1)}) custom-call(bf16[1,16,3584]{2,1,0:T(8,128)(2,1)} %down_ref.1, bf16[1,16,3584]{2,1,0:T(8,128)(2,1)} %up_ref.1, s32[2,2,16]{2,1,0:T(2,128)} %bitcast.7, f32[1,2,3584]{2,1,0:T(2,128)} %gains_ref.1, bf16[2,8,3584]{2,1,0:T(8,128)(2,1)} %bitcast.6, ...), custom_call_target="tpu_custom_call" | custom-call | tf_op jit(solution)/shard_map/routed_experts/pallas_call | solution.py:500
  88.6 0.6 copy.11
  89.3 0.6 copy.12

commit v4 on v3

--- a/solution.py
+++ b/solution.py
@@ -43,8 +43,9 @@
 
 
 def kernel(
-    down_ref, up_ref, routes_ref, gains_ref, router_ref, w_up_ref, w_down_ref,
+    down_hbm, up_hbm, routes_hbm, gains_hbm, router_hbm, w_up_ref, w_down_ref,
     out_down, out_up,
+    down_ref, up_ref, routes_ref, gains_ref, router_ref, in_local,
     tok, sel, sel2, got, got2, ans, ans2, mate, sum2, back, back2, part, part_in, acc, wu, wd, fin, fin_in,
     own_send, a_send, a_recv, b_send, b_recv, f_send, f_recv, m_send, m_recv, d_send, d_recv,
     e_send, e_recv, l_send, w_local, w_send, w_recv, z_send, z_recv,
@@ -84,6 +85,21 @@
     for friend in friends:
         pl.semaphore_signal(barrier, inc=1, device_id=friend, device_id_type=MESH)
 
+    inputs = [
+        pltpu.make_async_copy(src, dst, in_local.at[number])
+        for number, (src, dst) in enumerate(
+            (
+                (down_hbm, down_ref),
+                (up_hbm, up_ref),
+                (gains_hbm, gains_ref),
+                (router_hbm, router_ref),
+                (routes_hbm, routes_ref),
+            )
+        )
+    ]
+    for copy in inputs:
+        copy.start()
+
     def remote(src, dst, send, recv, device):
         return pltpu.make_async_remote_copy(
             src_ref=src, dst_ref=dst, send_sem=send, recv_sem=recv, device_id=device, device_id_type=MESH
@@ -112,6 +128,8 @@
     def put(first):
         return (iota((EXPERTS, META), 1) == iota((EXPERTS, META), 0) + first).astype(BF16)
 
+    for copy in inputs:
+        copy.wait()
     for side, state_ref in enumerate((down_ref, up_ref)):
         wide = state_ref[0].astype(F32)
         scale_rows = lax.rsqrt(jnp.mean(wide * wide, axis=-1, keepdims=True) + EPSILON)
@@ -330,6 +348,7 @@
         hit = (code == (c & 7).astype(F32)) & ((lax.shift_right_logical(c, 3) & 1) == lax.shift_right_logical(r, 4))
         high = jnp.where(hit, dot_lanes(info, spread(EXPERTS)), 0.0).astype(BF16)
         low = jnp.where(hit, dot_lanes(info, spread(2 * EXPERTS)), 0.0).astype(BF16)
+        both = jnp.concatenate([high, low], axis=0)
         for first in range(0, HALF, TILE):
             span = slice(first, first + TILE)
             answers = jnp.concatenate(
@@ -341,7 +360,8 @@
                 ],
                 axis=0,
             )
-            acc[half, :, span] = dot(high, answers) + dot(low, answers)
+            sums = dot(both, answers)
+            acc[half, :, span] = sums[0 : 2 * TOK] + sums[2 * TOK :]
 
     def e_copy(position, half):
         block, offset = index_at(position), offset_at(position)
@@ -421,8 +441,6 @@
             join(position, half)
             for side in range(2):
                 last_copy(position, half, side).start()
-
-    for half in range(2):
         combine(mine, half)
         span = slice(half * HALF, (half + 1) * HALF)
         for side, state_ref in enumerate((down_ref, up_ref)):
@@ -503,9 +521,15 @@
             pltpu.VMEM(state_down.shape, BF16),
             pltpu.VMEM(state_up.shape, BF16),
         ),
-        in_specs=[vmem] * 5 + [hbm] * 2,
+        in_specs=[hbm] * 7,
         out_specs=(vmem, vmem),
         scratch_shapes=[
+            pltpu.VMEM(state_down.shape, BF16),
+            pltpu.VMEM(state_up.shape, BF16),
+            pltpu.VMEM((2, 2, TOK), jnp.int32),
+            pltpu.VMEM(gains.shape, F32),
+            pltpu.VMEM((2, EXPERTS, D), BF16),
+            dma((5,)),
             pltpu.VMEM((BLOCKS, 2, 2 * TOK, WIDE), BF16),
             pltpu.VMEM((BLOCKS, 2, 2, TOK, HALF), BF16),
             pltpu.VMEM((BLOCKS, 2, TOK, HALF), BF16),

time: 90.1 us -> 88.8 us (0.986)
  Pallas kernels: 88 us -> 86.7 us
    pallas_call x1, Pallas kernels: 88 us -> 86.7 us  [on_device(): pl.pallas_call(kernel, out_shape=(pltpu.VMEM(state_down.shape, BF16), plt...]
where the time goes in v4:
time: 88.8 us; the launch traced here: 88.7 us
  Pallas kernels  86.7 us (98%)
  local copies, waits for them, and re-layouts  1.29 us (1%)
    pallas_call x1, Pallas kernels, on_device(): pl.pallas_call(kernel, out_shape=(pltpu.VMEM(state_down.shape, BF16), plt...  86.7 us

profile of v4, /device:TPU:64, one launch (start us, length us, event | category | flops | bytes accessed | tf_op | source)
XLA Modules:
  0.0 88.7 jit_solution(9731869384229938900)
XLA Ops:
  0.6 86.7 %routed_experts.1 = (bf16[1,16,3584]{2,1,0:T(8,128)(2,1)S(1)}, bf16[1,16,3584]{2,1,0:T(8,128)(2,1)S(1)}) custom-call(bf16[1,16,3584]{2,1,0:T(8,128)(2,1)} %down_hbm.1, bf16[1,16,3584]{2,1,0:T(8,128)(2,1)} %up_hbm.1, s32[2,2,16]{2,1,0:T(2,128)} %bitcast.7, f32[1,2,3584]{2,1,0:T(2,128)} %gains_hbm.1, bf16[2,8,3584]{2,1,0:T(8,128)(2,1)} %bitcast.6, ...), custom_call_target="tpu_custom_call" | custom-call | tf_op jit(solution)/shard_map/routed_experts/pallas_call | solution.py:518
  87.4 0.6 copy.11
  88.0 0.6 copy.12

commit v5 on v4

--- a/solution.py
+++ b/solution.py
@@ -151,6 +151,10 @@
         info = dot(code, put(0)) + dot(high, put(EXPERTS)) + dot(low, put(2 * EXPERTS))
         tok[mine, 0, own_rows, HALF:WIDE] = info.astype(BF16)
 
+    zeros_half = jnp.zeros((TOK, HALF), BF16)
+    for block in range(BLOCKS):
+        back2[block, other] = zeros_half
+
     pl.semaphore_wait(barrier, len(friends))
 
     def tok_at(block, half):
@@ -168,10 +172,6 @@
             own_copy(way, half).start()
     for index in range(4):
         weight_remote(index).start()
-
-    zeros_half = jnp.zeros((TOK, HALF), BF16)
-    for block in range(BLOCKS):
-        back2[block, other] = zeros_half
 
     rows = 4 * TOK
     row = iota((rows, META), 0)
@@ -239,7 +239,7 @@
             sel2[block, half, :, span] = picked[2 * TOK : 3 * TOK]
             sel[block, 1, half, :, span] = picked[3 * TOK :]
 
-    def experts(block):
+    def experts(block, at_once):
         total = jnp.zeros((rows, 4 * HID), F32)
         for half in range(2):
             lhs = jnp.concatenate(
@@ -260,6 +260,14 @@
                 ans2[block, half, :, span] = result[2 * TOK : 3 * TOK]
                 ans[block, 1, half, :, span] = result[3 * TOK :]
 
+            @pl.when(other == half)
+            def _():
+                m_copy(block).start()
+
+            @pl.when(at_once)
+            def _():
+                d_near(block, half)
+
     def d_near(block, half):
         for kind in range(2):
             d_copy(block, kind, half).start()
@@ -317,13 +325,7 @@
                 for kind in range(2):
                     b_copy(block, kind, half).wait_recv()
             f_wait(block)
-            experts(block)
-            m_copy(block).start()
-
-            @pl.when(step >= BLOCKS + LAG - 2)
-            def _():
-                d_near(block, 0)
-                d_near(block, 1)
+            experts(block, step >= BLOCKS + LAG - 2)
 
         @pl.when(step == BLOCKS)
         def _():

time: 88.8 us -> 88.9 us (level)
  no operation moved by 1% of the time
where the time goes in v5:
time: 88.9 us; the launch traced here: 88.7 us
  Pallas kernels  86.8 us (98%)
  local copies, waits for them, and re-layouts  1.29 us (1%)
    pallas_call x1, Pallas kernels, on_device(): pl.pallas_call(kernel, out_shape=(pltpu.VMEM(state_down.shape, BF16), plt...  86.8 us

profile of v5, /device:TPU:64, one launch (start us, length us, event | category | flops | bytes accessed | tf_op | source)
XLA Modules:
  0.0 88.7 jit_solution(14839207175385199980)
XLA Ops:
  0.6 86.8 %routed_experts.1 = (bf16[1,16,3584]{2,1,0:T(8,128)(2,1)S(1)}, bf16[1,16,3584]{2,1,0:T(8,128)(2,1)S(1)}) custom-call(bf16[1,16,3584]{2,1,0:T(8,128)(2,1)} %down_hbm.1, bf16[1,16,3584]{2,1,0:T(8,128)(2,1)} %up_hbm.1, s32[2,2,16]{2,1,0:T(2,128)} %bitcast.7, f32[1,2,3584]{2,1,0:T(2,128)} %gains_hbm.1, bf16[2,8,3584]{2,1,0:T(8,128)(2,1)} %bitcast.6, ...), custom_call_target="tpu_custom_call" | custom-call | tf_op jit(solution)/shard_map/routed_experts/pallas_call | solution.py:520
  87.4 0.6 copy.11
  88.1 0.6 copy.12
